TPU v7x, 512 devices: a whole 4x4x16 slice. The times are simulated.
512 devices in a mesh: region: 64 (over z, x), member: 8 (over y, core).
Axes of the slice: x: 4, y: 4, z: 16, core: 2. Of those that a mesh axis runs over, the one named last changes fastest.
Arguments:
- perturbations: bfloat16 [80, 2, 64, 8192], P('member', None, None, 'region'), may hold values from -0.65625 to 0.65625
- control: float32 [80, 64, 8192], P('member', None, 'region'), may hold values from -6 to 6
- vertical_loc: bfloat16 [64, 64], replicated, may hold values from -0.75 to 0.75
- block_kernels: bfloat16 [4, 128, 128], replicated, may hold values from -0.3125 to 0.3125
- loc_pattern: int32 [64, 3], replicated, may hold values from 0 to 3
- obs_region: int32 [65536, 1], P('region'), may hold values from 0 to 63; in each aligned block of 128 rows (0 to 127, 128 to 255, ...) at most 4 rows name the same one
- obs_slot: int32 [65536], P('region'), may hold values from 0 to 1
- obs_cell: int32 [65536], P('region'), may hold values from 0 to 127
- innovations: float32 [64, 65536], P(None, 'region'), may hold values from -12 to 12
- obs_weight: float32 [512, 128, 128], P('region'), may hold values from -0.0375 to 2, as said below
Outputs:
- analysis: float32 [80, 64, 8192], P('member', None, 'region')
Inputs may be any that keep to these rules, and one draw needn't show every extreme that they name: `obs_region`: in each aligned block of 128 rows, no region is named by more than 4 rows. `obs_weight`: each tile is symmetric, and in each row the diagonal entry exceeds the sum of the magnitudes of the other entries.
All inputs are finite; a program needn't handle non-finite values.
Results may differ from a plain program's by a relative error of at most 0.013.
Values may be sent and summed in bfloat16 or wider, within the bound.
A program may use at most 64 MiB of HBM per device.

v0:
```python
import jax
import jax.numpy as jnp
from jax import lax
from jax.sharding import PartitionSpec as P

SLOTS = 2
BLOCK = 128
TILE = 128
ITERS = 2
CELLS_DEV = 128
OBS_DEV = 1024


def padded_2(block, sides, width):
    for axis, dim in sides:
        count = lax.axis_size(axis)
        forward = [(i, i + 1) for i in range(count - 1)]
        backward = [(target, source) for source, target in forward]
        low = lax.ppermute(
            lax.slice_in_dim(block, block.shape[dim] - width, None, axis=dim), axis, forward
        )
        high = lax.ppermute(lax.slice_in_dim(block, 0, width, axis=dim), axis, backward)
        block = jnp.concatenate([low, block, high], axis=dim)
    return block


def pick_kernels(block_kernels, indices):
    kernel_ids = jnp.arange(block_kernels.shape[0], dtype=jnp.int32)
    onehot = (indices[:, None] == kernel_ids[None, :]).astype(jnp.bfloat16)
    return jnp.einsum(
        "bk,kij->bij", onehot, block_kernels, preferred_element_type=jnp.float32
    ).astype(jnp.bfloat16)


def spread_blocks(values, kernel_list, transposed):
    padded = padded_2(values, (("region", 2),), BLOCK)
    member_count, level_count, cell_count = values.shape
    block_count = cell_count // BLOCK
    summed = jnp.zeros((member_count, level_count, block_count, BLOCK), jnp.float32)
    for offset in range(3):
        first_cell = (2 - offset) * BLOCK if transposed else offset * BLOCK
        window = padded[:, :, first_cell : first_cell + cell_count].reshape(
            member_count, level_count, block_count, BLOCK
        )
        if transposed:
            summed = summed + jnp.einsum(
                "mlbj,bkj->mlbk", window, kernel_list[offset], preferred_element_type=jnp.float32
            )
        else:
            summed = summed + jnp.einsum(
                "mlbk,bkj->mlbj", window, kernel_list[offset], preferred_element_type=jnp.float32
            )
    return summed.reshape(member_count, level_count, cell_count)


def route_rows(targets, sub_count, regions, capacity):
    obs_total = targets.shape[0]
    per_sub = obs_total // sub_count
    grouped = targets.reshape(sub_count, per_sub)
    region_ids = jnp.arange(regions, dtype=jnp.int32)
    onehot = (grouped[:, :, None] == region_ids[None, None, :]).astype(jnp.int32)
    before = jnp.cumsum(onehot, axis=1) - onehot
    ranking = jnp.sum(before * onehot, axis=2)
    sub_index = jnp.arange(sub_count, dtype=jnp.int32)[:, None]
    position = (grouped * (sub_count * capacity) + sub_index * capacity + ranking).reshape(
        obs_total
    )
    slot_row = jnp.full((regions * sub_count * capacity,), obs_total, jnp.int32)
    slot_row = slot_row.at[position].set(jnp.arange(obs_total, dtype=jnp.int32))
    return (position, slot_row)


def squared_norm(vector):
    return lax.psum(jnp.sum(vector * vector), ("region", "member"))


def local(
    perturbations,
    control,
    vertical_loc,
    block_kernels,
    loc_pattern,
    obs_region,
    obs_slot,
    obs_cell,
    innovations,
    obs_weight,
):
    regions = lax.axis_size("region")
    members = lax.axis_size("member")
    region_index = lax.axis_index("region")
    member_index = lax.axis_index("member")
    nblocks = CELLS_DEV // BLOCK
    capacity = max(2, 2 * (OBS_DEV // members) // regions)
    group_rows = OBS_DEV // members
    pattern_pad = jnp.pad(loc_pattern, ((1, 1), (0, 0)))
    pattern_rows = lax.dynamic_slice_in_dim(pattern_pad, region_index * nblocks, nblocks + 2, 0)
    forward_list = [
        pick_kernels(block_kernels, pattern_rows[1 : nblocks + 1, offset]) for offset in range(3)
    ]
    backward_list = [
        pick_kernels(block_kernels, pattern_rows[2 - offset : 2 - offset + nblocks, offset])
        for offset in range(3)
    ]
    cell_codes = obs_slot * CELLS_DEV + obs_cell
    targets = obs_region[:, 0]
    sub_count = 1
    first_row = member_index * group_rows
    targets = lax.dynamic_slice_in_dim(targets, first_row, group_rows, 0)
    obs_codes = lax.dynamic_slice_in_dim(cell_codes, first_row, group_rows, 0)
    innovation_rows = lax.dynamic_slice_in_dim(innovations, first_row, group_rows, 1)
    weight_tiles = lax.dynamic_slice_in_dim(
        obs_weight, member_index * (group_rows // TILE), group_rows // TILE, 0
    )
    position, slot_row = route_rows(targets, sub_count, regions, capacity)
    padded_codes = jnp.concatenate([obs_codes, jnp.full((1,), SLOTS * CELLS_DEV, jnp.int32)])
    region_codes = lax.all_to_all(
        padded_codes[slot_row], "region", split_axis=0, concat_axis=0, tiled=True
    )

    def apply_operator(vector, with_innovation):
        spread = spread_blocks(vector.astype(jnp.bfloat16), forward_list, False).astype(
            jnp.bfloat16
        )
        weights = jnp.einsum(
            "lk,mkc->mlc", vertical_loc, spread, preferred_element_type=jnp.float32
        )
        member_sum = jnp.sum(perturbations.astype(jnp.float32) * weights[:, None], axis=0)
        increment = lax.psum(member_sum.astype(jnp.bfloat16), "member").astype(jnp.float32)
        levels_here = increment.shape[1]
        flattened = increment.transpose(1, 0, 2).reshape(levels_here, SLOTS * CELLS_DEV)
        flat_padded = jnp.concatenate([flattened, jnp.zeros((levels_here, 1), jnp.float32)], axis=1)
        sampled = jnp.take(flat_padded, region_codes, axis=1)
        at_holders = lax.all_to_all(
            sampled.astype(jnp.bfloat16), "region", split_axis=1, concat_axis=1, tiled=True
        ).astype(sampled.dtype)
        departures = jnp.take(at_holders, position, axis=1)
        if with_innovation:
            departures = departures - innovation_rows
        obs_count = departures.shape[1]
        weighted = jnp.einsum(
            "ltk,tkj->ltj",
            departures.reshape(levels_here, obs_count // TILE, TILE),
            weight_tiles,
            precision=lax.Precision.HIGHEST,
        ).reshape(levels_here, obs_count)
        weighted_pad = jnp.concatenate([weighted, jnp.zeros((levels_here, 1), jnp.float32)], axis=1)
        returned = jnp.take(weighted_pad, slot_row, axis=1)
        at_regions = lax.all_to_all(
            returned.astype(jnp.bfloat16), "region", split_axis=1, concat_axis=1, tiled=True
        ).astype(returned.dtype)
        adjoint_flat = (
            jnp.zeros((levels_here, SLOTS * CELLS_DEV + 1), jnp.float32)
            .at[:, region_codes]
            .add(at_regions)
        )
        adjoint_part = (
            adjoint_flat[:, : SLOTS * CELLS_DEV]
            .reshape(levels_here, SLOTS, CELLS_DEV)
            .transpose(1, 0, 2)
        )
        adjoint_field = lax.psum(adjoint_part.astype(jnp.bfloat16), "member").astype(jnp.float32)
        projected = jnp.sum(perturbations.astype(jnp.float32) * adjoint_field[None], axis=1).astype(
            jnp.bfloat16
        )
        lifted = jnp.einsum(
            "kl,mkc->mlc", vertical_loc, projected, preferred_element_type=jnp.float32
        ).astype(jnp.bfloat16)
        return vector + spread_blocks(lifted, backward_list, True)

    solution = control
    residual = -apply_operator(control, True)
    direction = residual
    norm_now = squared_norm(residual)
    for iteration in range(ITERS):
        curved = apply_operator(direction, False)
        step_size = norm_now / lax.psum(jnp.sum(direction * curved), ("region", "member"))
        solution = solution + step_size * direction
        if iteration + 1 < ITERS:
            residual = residual - step_size * curved
            norm_next = squared_norm(residual)
            direction = residual + norm_next / norm_now * direction
            norm_now = norm_next
    return solution


def solution(mesh):
    placed = (
        P("member", None, None, "region"),
        P("member", None, "region"),
        P(),
        P(),
        P(),
        P("region", None),
        P("region"),
        P("region"),
        P(None, "region"),
        P("region", None, None),
    )
    return jax.shard_map(
        local, mesh=mesh, in_specs=placed, out_specs=P("member", None, "region"), check_vma=False
    )
```

profile of v0, /device:TPU:1, one launch (start us, length us, event | category | flops | bytes accessed | tf_op | source)
XLA Modules:
  0.0 704.8 jit_solution(5784242501238272621)
XLA Ops:
  2.4 4.6 collective-permute-start
  12.6 20.4 %all-to-all-start = ((s32[64,4,1]{1,2,0:T(1,128)}), s32[64,4,1]{1,2,0:T(1,128)S(1)}, u32[]{:S(2)}, u32[]{:S(2)}) async-start(s32[64,4,1]{1,2,0:T(1,128)} %bitcast.8), calls=%async_computation | async-start | bytes 65536 | tf_op jit(solution)/shard_map/all_to_all | solution.py:117
  39.4 6.9 all-to-all-done
  48.4 23.6 %psum.70 = bf16[64,256]{0,1:T(8,128)(2,1)S(1)} all-reduce(bf16[64,256]{0,1:T(8,128)(2,1)S(1)} %bitcast.318), channel_id=1, replica_groups=mesh['region'=64,'member'=8] {'member'}, use_global_device_ids=true, to_apply=%region_4.5 | all-reduce | flops 16384 | bytes 65536 | tf_op jit(solution)/shard_map/psum | solution.py:129
  73.7 7.5 %all-to-all-start.1 = ((bf16[64,2,128]{2,1,0:T(2,128)(2,1)}), bf16[64,2,128]{2,1,0:T(2,128)(2,1)S(1)}, u32[]{:S(2)}, u32[]{:S(2)}) async-start(bf16[64,2,128]{2,1,0:T(2,128)(2,1)} %reshape.599), calls=%async_computation.1 | async-start | bytes 65536 | tf_op jit(solution)/shard_map/all_to_all | solution.py:134
  83.6 11.0 %all-to-all-done.1 = bf16[64,2,128]{2,1,0:T(2,128)(2,1)S(1)} async-done(((bf16[64,2,128]{2,1,0:T(2,128)(2,1)}), bf16[64,2,128]{2,1,0:T(2,128)(2,1)S(1)}, u32[]{:S(2)}, u32[]{:S(2)}) %all-to-all-start.1) | async-done | bytes 32800 | tf_op jit(solution)/shard_map/all_to_all | solution.py:134
  97.5 4.6 all-to-all-start.2
  102.1 13.5 %all-to-all-done.2 = bf16[64,2,128]{2,1,0:T(2,128)(2,1)S(1)} async-done(((bf16[64,2,128]{2,1,0:T(2,128)(2,1)}), bf16[64,2,128]{2,1,0:T(2,128)(2,1)S(1)}, u32[]{:S(2)}, u32[]{:S(2)}) %all-to-all-start.2) | async-done | bytes 32800 | tf_op jit(solution)/shard_map/all_to_all | solution.py:149
  117.3 26.2 %psum.71 = bf16[2,64,128]{2,1,0:T(8,128)(2,1)S(1)} all-reduce(bf16[2,64,128]{2,1,0:T(8,128)(2,1)S(1)} %bitcast.328), channel_id=1, replica_groups=mesh['region'=64,'member'=8] {'member'}, use_global_device_ids=true, to_apply=%region_6.10 | all-reduce | flops 16384 | bytes 65536 | tf_op jit(solution)/shard_map/psum | solution.py:162
  148.4 3.6 collective-permute-done.2
  153.5 4.0 collective-permute-start.4
  160.3 26.9 %psum.73 = bf16[64,256]{0,1:T(8,128)(2,1)S(1)} all-reduce(bf16[64,256]{0,1:T(8,128)(2,1)S(1)} %bitcast.322), channel_id=1, replica_groups=mesh['region'=64,'member'=8] {'member'}, use_global_device_ids=true, to_apply=%region_11.15 | all-reduce | flops 16384 | bytes 65536 | tf_op jit(solution)/shard_map/psum | solution.py:129
  188.3 27.9 %all_to_all.69 = bf16[64,2,128]{2,1,0:T(2,128)(2,1)S(1)} all-to-all(bf16[64,2,128]{2,1,0:T(2,128)(2,1)S(1)} %reshape.603), channel_id=1, replica_groups=mesh['region'=64,'member'=8] {'region'}, dimensions={0} | all-to-all | bytes 65536 | tf_op jit(solution)/shard_map/all_to_all | solution.py:134
  218.5 17.4 %all_to_all.70 = bf16[64,2,128]{2,1,0:T(2,128)(2,1)S(1)} all-to-all(bf16[64,2,128]{2,1,0:T(2,128)(2,1)S(1)} %reshape.605), channel_id=1, replica_groups=mesh['region'=64,'member'=8] {'region'}, dimensions={0} | all-to-all | bytes 65536 | tf_op jit(solution)/shard_map/all_to_all | solution.py:149
  237.6 25.9 %psum.74 = bf16[2,64,128]{2,1,0:T(8,128)(2,1)S(1)} all-reduce(bf16[2,64,128]{2,1,0:T(8,128)(2,1)S(1)} %bitcast.329), channel_id=1, replica_groups=mesh['region'=64,'member'=8] {'member'}, use_global_device_ids=true, to_apply=%region_13.17 | all-reduce | flops 16384 | bytes 65536 | tf_op jit(solution)/shard_map/psum | solution.py:162
  273.0 106.0 %all-reduce.7 = (f32[]{:T(128)}, f32[]{:T(128)}) all-reduce(f32[]{:T(128)} %get-tuple-element.8, f32[]{:T(128)} %get-tuple-element.6), channel_id=1, replica_groups=mesh['region'=64,'member'=8] {'region','member'}, use_global_device_ids=true, to_apply=%region_9.13 | all-reduce | flops 2 | bytes 16 | tf_op jit(solution)/shard_map/psum | solution.py:74
  380.9 99.5 %psum.76 = f32[]{:T(128)} all-reduce(f32[]{:T(128)} %multiply_reduce_fusion), channel_id=1, replica_groups=mesh['region'=64,'member'=8] {'region','member'}, use_global_device_ids=true, to_apply=%region_18.22 | all-reduce | flops 1 | bytes 8 | tf_op jit(solution)/shard_map/psum | solution.py:74
  483.0 4.0 collective-permute-start.8
  490.1 22.6 %psum.77 = bf16[64,256]{0,1:T(8,128)(2,1)S(1)} all-reduce(bf16[64,256]{0,1:T(8,128)(2,1)S(1)} %bitcast.326), channel_id=1, replica_groups=mesh['region'=64,'member'=8] {'member'}, use_global_device_ids=true, to_apply=%region_20.24 | all-reduce | flops 16384 | bytes 65536 | tf_op jit(solution)/shard_map/psum | solution.py:129
  513.8 26.2 %all_to_all.71 = bf16[64,2,128]{2,1,0:T(2,128)(2,1)S(1)} all-to-all(bf16[64,2,128]{2,1,0:T(2,128)(2,1)S(1)} %reshape.607), channel_id=1, replica_groups=mesh['region'=64,'member'=8] {'region'}, dimensions={0} | all-to-all | bytes 65536 | tf_op jit(solution)/shard_map/all_to_all | solution.py:134
  542.3 17.4 %all_to_all.72 = bf16[64,2,128]{2,1,0:T(2,128)(2,1)S(1)} all-to-all(bf16[64,2,128]{2,1,0:T(2,128)(2,1)S(1)} %reshape.609), channel_id=1, replica_groups=mesh['region'=64,'member'=8] {'region'}, dimensions={0} | all-to-all | bytes 65536 | tf_op jit(solution)/shard_map/all_to_all | solution.py:149
  561.4 25.9 %psum.78 = bf16[2,64,128]{2,1,0:T(8,128)(2,1)S(1)} all-reduce(bf16[2,64,128]{2,1,0:T(8,128)(2,1)S(1)} %bitcast.330), channel_id=1, replica_groups=mesh['region'=64,'member'=8] {'member'}, use_global_device_ids=true, to_apply=%region_22.26 | all-reduce | flops 16384 | bytes 65536 | tf_op jit(solution)/shard_map/psum | solution.py:162
  592.2 3.6 collective-permute-done.10
  596.8 105.8 %psum.79 = f32[]{:T(128)} all-reduce(f32[]{:T(128)} %fusion.28), channel_id=1, replica_groups=mesh['region'=64,'member'=8] {'region','member'}, use_global_device_ids=true, to_apply=%region_25.29 | all-reduce | flops 1 | bytes 8 | tf_op jit(solution)/shard_map/psum | solution.py:177
  (158 shorter events, 65.4 us)
Async XLA Ops:
  0.0 95.3 %copy-start = (f32[8,128,128]{2,1,0:T(8,128)S(1)}, f32[8,128,128]{2,1,0:T(8,128)}, u32[]{:S(2)}) copy-start(f32[8,128,128]{2,1,0:T(8,128)} %param.25) | copy-start | bytes 1572868
  1.1 45.4 %collective-permute-start.1 = (bf16[10,64,128]{2,1,0:T(8,128)(2,1)S(1)}, bf16[10,64,128]{2,1,0:T(8,128)(2,1)S(1)}, u32[]{:S(2)}, u32[]{:S(2)}) collective-permute-start(bf16[10,64,128]{2,1,0:T(8,128)(2,1)S(1)} %convert_element_type.222), channel_id=1, source_target_pairs={{8,0},{16,8},{24,16},{32,24},{40,32},{48,40},{56,48},{64,56},{72,6... | collective-permute-start | bytes 491528 | tf_op jit(solution)/shard_map/ppermute | solution.py:22
  2.4 44.3 %collective-permute-start = (bf16[10,64,128]{2,1,0:T(8,128)(2,1)S(1)}, bf16[10,64,128]{2,1,0:T(8,128)(2,1)S(1)}, u32[]{:S(2)}, u32[]{:S(2)}) collective-permute-start(bf16[10,64,128]{2,1,0:T(8,128)(2,1)S(1)} %convert_element_type.222), channel_id=1, source_target_pairs={{0,8},{8,16},{16,24},{24,32},{32,40},{40,48},{48,56},{56,64},{64,7... | collective-permute-start | bytes 491528 | tf_op jit(solution)/shard_map/ppermute | solution.py:19
  7.0 0.7 copy-start.5
  7.0 0.7 copy-start.4
  9.9 25.2 %copy-start.7 = (bf16[4,128,128]{2,1,0:T(8,128)(2,1)S(1)}, bf16[4,128,128]{2,1,0:T(8,128)(2,1)}, u32[]{:S(2)}) copy-start(bf16[4,128,128]{2,1,0:T(8,128)(2,1)} %param.19) | copy-start | bytes 393220
  12.6 33.7 %all-to-all-start = ((s32[64,4,1]{1,2,0:T(1,128)}), s32[64,4,1]{1,2,0:T(1,128)S(1)}, u32[]{:S(2)}, u32[]{:S(2)}) async-start(s32[64,4,1]{1,2,0:T(1,128)} %bitcast.8), calls=%async_computation | async-start | bytes 65536 | tf_op jit(solution)/shard_map/all_to_all | solution.py:117
  33.6 0.7 copy-start.6
  46.5 0.7 copy-start.3
  47.2 1.0 copy-start.1
  73.7 20.9 %all-to-all-start.1 = ((bf16[64,2,128]{2,1,0:T(2,128)(2,1)}), bf16[64,2,128]{2,1,0:T(2,128)(2,1)S(1)}, u32[]{:S(2)}, u32[]{:S(2)}) async-start(bf16[64,2,128]{2,1,0:T(2,128)(2,1)} %reshape.599), calls=%async_computation.1 | async-start | bytes 65536 | tf_op jit(solution)/shard_map/all_to_all | solution.py:134
  97.5 18.1 %all-to-all-start.2 = ((bf16[64,2,128]{2,1,0:T(2,128)(2,1)}), bf16[64,2,128]{2,1,0:T(2,128)(2,1)S(1)}, u32[]{:S(2)}, u32[]{:S(2)}) async-start(bf16[64,2,128]{2,1,0:T(2,128)(2,1)} %reshape.601), calls=%async_computation.2 | async-start | bytes 65536 | tf_op jit(solution)/shard_map/all_to_all | solution.py:149
  143.8 4.3 collective-permute-start.3
  145.9 6.1 collective-permute-start.2
  147.4 4.6 copy-start.2
  152.2 6.1 collective-permute-start.5
  153.5 6.2 collective-permute-start.4
  263.8 4.4 collective-permute-start.7
  266.0 6.1 collective-permute-start.6
  481.7 7.0 collective-permute-start.9
  483.0 6.5 collective-permute-start.8
  587.6 4.4 collective-permute-start.11
  589.8 6.1 collective-permute-start.10
where the time goes:
time: 707 us; the launch traced here: 705 us
  blocking collectives  551 us (78%)
  starting transfers between devices  59.2 us (8%)
  waiting for transfers between devices  48.5 us (7%)
  local copies, waits for them, and re-layouts  19.2 us (3%)
  matrix products  11.3 us (2%)
  other arithmetic  10.9 us (2%)
    psum x2, blocking collectives, squared_norm(): return lax.psum(jnp.sum(vector * vector), ('region', 'member'))  205 us
    psum x1, blocking collectives, local(): lax.psum(jnp.sum(direction * curved), ('region', 'member'))  106 us
    psum x3, blocking collectives, apply_operator(): lax.psum(adjoint_part.astype(jnp.bfloat16), 'member').astype(jnp.float32)  77.9 us
    psum x3, blocking collectives, apply_operator(): lax.psum(member_sum.astype(jnp.bfloat16), 'member').astype(jnp.float32)  73.1 us
    all_to_all x2, blocking collectives, apply_operator(): lax.all_to_all(sampled.astype(jnp.bfloat16), 'region', split_axis=1, conc...  54.1 us
    all_to_all x2, blocking collectives, apply_operator(): lax.all_to_all(returned.astype(jnp.bfloat16), 'region', split_axis=1, con...  34.7 us
    all_to_all x1, starting transfers between devices, local(): lax.all_to_all(padded_codes[slot_row], 'region', split_axis=0, concat_axi...  20.4 us
    ppermute x6, starting transfers between devices, padded_2(): lax.ppermute(lax.slice_in_dim(block, block.shape[dim] - width, None, axis...  19 us
  transfers between devices with their start and end apart: 15, of which 13 were waited for; matrix products, arithmetic and copies ran while one was open for 2% of the time, Pallas kernels for 0%

commit v1 on v0

v1 whole, which is shorter than its diff:
```python
import jax
import jax.numpy as jnp
from jax import lax
from jax.experimental import pallas as pl
from jax.experimental.pallas import tpu as pltpu
from jax.sharding import PartitionSpec as P

REGIONS, MEMBERS = 64, 8
OWN = 10
LEV, CELLS = 64, 128
ROWS = OWN * LEV
TILES = 8
LPM = LEV // MEMBERS
KTYPES = 4
F32, BF16 = jnp.float32, jnp.bfloat16
MESH = pl.DeviceIdType.MESH
CODES, SAMPLES, RETURNS, SCALARS = 0, (1, 3, 5), (2, 4), 6
SUMS, ADJOINTS, MEMBER_SCALARS = (0, 2, 4), (1, 3), 5
VECTORS, LIFTED = (0, 2, 4), (1, 3)


def dot(a, b):
    return jnp.dot(a, b, preferred_element_type=F32)


def dot_nt(a, b):
    return lax.dot_general(a, b, (((1,), (1,)), ((), ())), preferred_element_type=F32)


def bit_of(shape, axis, stride):
    return (lax.broadcasted_iota(jnp.int32, shape, axis) & stride) != 0


def swap_bits(x, row_stride, lane_stride):
    n = x.shape[0]
    row, lane = bit_of(x.shape, 0, row_stride), bit_of(x.shape, 1, lane_stride)
    up = pltpu.roll(pltpu.roll(x, n - row_stride, 0), lane_stride, 1)
    down = pltpu.roll(pltpu.roll(x, row_stride, 0), CELLS - lane_stride, 1)
    return jnp.where(row == lane, x, jnp.where(row, down, up))


def region_major(x):
    return swap_bits(swap_bits(x, 2, 32), 4, 64)


def tile_major(x):
    return swap_bits(swap_bits(swap_bits(x, 8, 4), 16, 8), 32, 16)


def split(x):
    high = x.astype(BF16)
    return high, (x - high.astype(F32)).astype(BF16)


def kernel(
    pert_ref, control_ref, vloc_ref, table_ref, pattern_ref, region_ref, code_ref, innov_ref, weight_ref,
    out_ref,
    pert, weight, innov, r0, q, halo_out, halo_in, own_lift,
    cols_out, cols_in, part_out, part_in,
    onehot, coupling, innov_slots, blocks, vert,
    load_sem, bar_done, col_send, col_recv, part_send, part_recv, halo_send, halo_recv,
):
    region, member = lax.axis_index("region"), lax.axis_index("member")
    left, right = lax.rem(region + (REGIONS - 1), REGIONS), lax.rem(region + 1, REGIONS)

    loads = [
        pltpu.make_async_copy(pert_ref, pert, load_sem.at[0]),
        pltpu.make_async_copy(weight_ref, weight, load_sem.at[1]),
        pltpu.make_async_copy(innov_ref.at[pl.ds(pl.multiple_of(member * LPM, LPM), LPM)], innov, load_sem.at[2]),
    ]
    barrier = pltpu.get_barrier_semaphore()

    def greet_region(i, _):
        pl.semaphore_signal(
            barrier, inc=1, device_id={"region": lax.rem(region + i, REGIONS)}, device_id_type=MESH
        )
        return 0

    lax.fori_loop(1, REGIONS, greet_region, 0)

    def greet_member(i, _):
        pl.semaphore_signal(
            barrier, inc=1, device_id={"member": lax.rem(member + i, MEMBERS)}, device_id_type=MESH
        )
        return 0

    lax.fori_loop(1, MEMBERS, greet_member, 0)
    for load in (loads[1], loads[2], loads[0]):
        load.start()

    def start_columns(n):
        def one(i):
            to = lax.rem(region + i, REGIONS)
            pltpu.make_async_remote_copy(
                src_ref=cols_out.at[n, to], dst_ref=cols_in.at[n, region],
                send_sem=col_send.at[n], recv_sem=col_recv.at[n],
                device_id={"region": to}, device_id_type=MESH,
            ).start()

        def pair(j, _):
            one(32 - j)
            one(32 + j)
            return 0

        one(32)
        lax.fori_loop(1, 32, pair, 0)

    def columns_like(n):
        return pltpu.make_async_remote_copy(
            src_ref=cols_out.at[n, pl.ds(0, REGIONS - 1)], dst_ref=cols_in.at[n, pl.ds(0, REGIONS - 1)],
            send_sem=col_send.at[n], recv_sem=col_recv.at[n],
            device_id={"region": right}, device_id_type=MESH,
        )

    def start_parts(n, same):
        def one(i, _):
            to = lax.rem(member + i, MEMBERS)
            pltpu.make_async_remote_copy(
                src_ref=part_out.at[n, member if same else to], dst_ref=part_in.at[n, member],
                send_sem=part_send.at[n], recv_sem=part_recv.at[n],
                device_id={"member": to}, device_id_type=MESH,
            ).start()
            return 0

        lax.fori_loop(1, MEMBERS, one, 0)

    def parts_like(n):
        return pltpu.make_async_remote_copy(
            src_ref=part_out.at[n, pl.ds(0, MEMBERS - 1)], dst_ref=part_in.at[n, pl.ds(0, MEMBERS - 1)],
            send_sem=part_send.at[n], recv_sem=part_recv.at[n],
            device_id={"member": lax.rem(member + 1, MEMBERS)}, device_id_type=MESH,
        )

    def halo(n, side):
        return pltpu.make_async_remote_copy(
            src_ref=halo_out.at[n], dst_ref=halo_in.at[n, 1 - side],
            send_sem=halo_send.at[n, side], recv_sem=halo_recv.at[n, 1 - side],
            device_id={"region": left if side == 0 else right}, device_id_type=MESH,
        )

    def wait_halo(n, side):
        pltpu.make_async_remote_copy(
            src_ref=halo_out.at[n], dst_ref=halo_in.at[n, side],
            send_sem=halo_send.at[n, 1 - side], recv_sem=halo_recv.at[n, side],
            device_id={"region": left if side == 0 else right}, device_id_type=MESH,
        ).wait_recv()

    def send_columns(n, x):
        cols_out[n] = region_major(x).reshape(REGIONS, 2, CELLS)
        cols_in[n, region] = cols_out[n, region]
        start_columns(n)

    def get_columns(n):
        columns_like(n).wait_recv()
        return region_major(cols_in[n].reshape(2 * REGIONS, CELLS))

    halo_out[VECTORS[0]] = control_ref[...].astype(BF16)

    regions8 = region_ref[...]
    codes8 = code_ref[...].astype(F32).astype(BF16)
    iota_row = lax.broadcasted_iota(jnp.int32, (CELLS, CELLS), 0)
    iota_lane = lax.broadcasted_iota(jnp.int32, (CELLS, CELLS), 1)
    identity = (iota_row == iota_lane).astype(F32).astype(BF16)
    zz, xx = regions8 >> 2, regions8 & 3
    base8 = 128 * (zz >> 3) + 32 * xx + 4 * (zz & 7)
    base_cols = dot_nt(identity, base8.astype(F32).astype(BF16)).astype(jnp.int32)
    slot_lane = lax.broadcasted_iota(jnp.int32, (CELLS, 2 * CELLS), 1)
    slot_row = lax.broadcasted_iota(jnp.int32, (2 * CELLS, CELLS), 0)
    tile_rows = lax.broadcasted_iota(jnp.int32, (8, 2 * CELLS), 0)
    code_halves = [[], []]
    placing, placing_t = [], []
    for t in range(TILES):
        col, row = base_cols[:, t : t + 1], base8[t : t + 1, :]
        same = col == row
        rank_col = jnp.sum((same & (iota_lane < iota_row)).astype(F32), axis=1, keepdims=True)
        rank_row = jnp.sum((same & (iota_row < iota_lane)).astype(F32), axis=0, keepdims=True)
        place = (slot_lane == col + rank_col.astype(jnp.int32)).astype(F32).astype(BF16)
        place_t = (slot_row == row + rank_row.astype(jnp.int32)).astype(F32).astype(BF16)
        placing.append(place)
        placing_t.append(place_t)
        codes = dot(codes8, place)
        codes = jnp.sum(jnp.where(tile_rows == t, codes, 0.0), axis=0, keepdims=True)
        codes = jnp.broadcast_to(codes, (8, 2 * CELLS))
        code_halves[0].append(codes[:, :CELLS])
        code_halves[1].append(codes[:, CELLS:])
    code_rows = tile_major(jnp.concatenate(code_halves[0] + code_halves[1], axis=0))

    pl.semaphore_wait(barrier, REGIONS - 1 + MEMBERS - 1)
    halo(VECTORS[0], 0).start()
    halo(VECTORS[0], 1).start()
    send_columns(CODES, code_rows)

    def block_of(at, offset):
        inside = (at >= 0) & (at < REGIONS)
        entry = pattern_ref[jnp.clip(at, 0, REGIONS - 1), offset]
        entry = jnp.where(inside, entry, -1)
        total = jnp.zeros((CELLS, CELLS), F32)
        for k in range(KTYPES):
            total = total + table_ref[k].astype(F32) * (entry == k).astype(F32)
        return total.astype(BF16)

    for side in range(3):
        present = (region + side - 1 >= 0) & (region + side - 1 < REGIONS)
        keep = present.astype(F32)
        blocks[0, side] = (block_of(region, side).astype(F32) * keep).astype(BF16)
        back = block_of(region + side - 1, 2 - side)
        blocks[1, side] = dot_nt(identity, back).astype(BF16)
    zeros = jnp.zeros((LEV, LEV), BF16)
    vloc = vloc_ref[...]
    vloc_t = dot_nt(identity[:LEV, :LEV], vloc).astype(BF16)
    for i, v in enumerate((vloc, vloc_t)):
        vert[i] = jnp.concatenate(
            [jnp.concatenate([v, zeros], axis=1), jnp.concatenate([zeros, v], axis=1)], axis=0
        )

    loads[1].wait()
    loads[2].wait()
    for t in range(TILES):
        for i, part in enumerate(split(weight[t])):
            coupling[i, t] = dot(placing_t[t], dot(part, placing[t]).astype(BF16)).astype(BF16)
        high, low = split(innov[:, CELLS * t : CELLS * (t + 1)])
        innov_slots[t] = dot(high, placing[t]) + dot(low, placing[t])

    codes = get_columns(CODES)
    code_row = lax.broadcasted_iota(jnp.int32, (2 * CELLS, CELLS), 0)
    for z in range(16):
        want = codes[8 * z : 8 * z + 1, :].astype(jnp.int32) - 1
        onehot[:, CELLS * z : CELLS * (z + 1)] = (code_row == want).astype(F32).astype(BF16)
    loads[0].wait()

    def conv(which, n):
        return (
            dot(halo_in[n, 0], blocks[which, 0])
            + dot(halo_out[n], blocks[which, 1])
            + dot(halo_in[n, 1], blocks[which, 2])
        )

    def forward(it):
        n = VECTORS[it]
        wait_halo(n, 0)
        wait_halo(n, 1)
        spread = conv(0, n).astype(BF16)
        sums = [jnp.zeros((LEV, CELLS), F32) for _ in range(2)]
        for pair in range(OWN // 2):
            local = dot(vert[0], spread[128 * pair : 128 * (pair + 1)])
            for i in range(2):
                for s in range(2):
                    sums[s] = sums[s] + pert[2 * pair + i, s].astype(F32) * local[LEV * i : LEV * (i + 1)]
        n = SUMS[it]
        for to in range(MEMBERS):
            for s in range(2):
                part_out[n, to, LPM * s : LPM * (s + 1)] = sums[s][LPM * to : LPM * (to + 1)]
        part_in[n, member] = part_out[n, member]
        start_parts(n, False)
        parts_like(n).wait_recv()
        total = jnp.sum(part_in[n], axis=0)
        increment = jnp.concatenate([total[:LPM], total[LPM:]], axis=1).astype(BF16)
        sampled = dot(increment, onehot[...])
        send_columns(
            SAMPLES[it], jnp.concatenate([sampled[:, CELLS * z : CELLS * (z + 1)] for z in range(16)], axis=0)
        )

    def weighted(it):
        slots = tile_major(get_columns(SAMPLES[it]))
        departures, results = [], []
        for t in range(TILES):
            here = jnp.concatenate([slots[8 * t : 8 * t + 8], slots[64 + 8 * t : 72 + 8 * t]], axis=1)
            if it == 0:
                here = here - innov_slots[t]
                high, low = split(here)
                result = dot(high, coupling[0, t]) + dot(low, coupling[0, t]) + dot(high, coupling[1, t])
            else:
                high = here.astype(BF16)
                result = dot(high, coupling[0, t]) + dot(high, coupling[1, t])
            departures.append(here)
            results.append(result)
        return departures, results

    def backward(it, results):
        back = jnp.concatenate([x[:, :CELLS] for x in results] + [x[:, CELLS:] for x in results], axis=0)
        send_columns(RETURNS[it], tile_major(back))
        here = get_columns(RETURNS[it]).astype(BF16)
        here = jnp.concatenate([here[8 * z : 8 * z + 8] for z in range(16)], axis=1)
        adjoint = dot_nt(here, onehot[...])
        n = ADJOINTS[it]
        mine = jnp.concatenate([adjoint[:, :CELLS], adjoint[:, CELLS:]], axis=0)
        part_out[n, member] = mine
        part_in[n, member] = mine
        start_parts(n, True)
        parts_like(n).wait_recv()
        fields = part_in[n]
        fields = [fields[:, LPM * s : LPM * (s + 1)].reshape(LEV, CELLS) for s in range(2)]
        n = LIFTED[it]
        for pair in range(OWN // 2):
            projected = jnp.concatenate(
                [
                    pert[k, 0].astype(F32) * fields[0] + pert[k, 1].astype(F32) * fields[1]
                    for k in (2 * pair, 2 * pair + 1)
                ],
                axis=0,
            ).astype(BF16)
            halo_out[n, 128 * pair : 128 * (pair + 1)] = dot(vert[1], projected).astype(BF16)
        halo(n, 0).start()
        halo(n, 1).start()
        wait_halo(n, 0)
        wait_halo(n, 1)
        return conv(1, n)

    forward(0)
    _, results = weighted(0)
    first = -(control_ref[...] + backward(0, results))
    r0[...] = first
    halo_out[VECTORS[1]] = first.astype(BF16)
    halo(VECTORS[1], 0).start()
    halo(VECTORS[1], 1).start()

    forward(1)
    _, results = weighted(1)
    second = r0[...] + backward(1, results)
    q[...] = second
    halo_out[VECTORS[2]] = second.astype(BF16)
    halo(VECTORS[2], 0).start()
    halo(VECTORS[2], 1).start()

    forward(2)
    departures, results = weighted(2)
    curve = sum(jnp.sum(d * w, axis=0, keepdims=True) for d, w in zip(departures, results, strict=True))
    curve = curve[:, :CELLS] + curve[:, CELLS:]
    first, second = r0[...], q[...]
    rows = [
        jnp.sum(first * first, axis=0, keepdims=True),
        jnp.sum(first * second, axis=0, keepdims=True),
        jnp.sum(second * second, axis=0, keepdims=True),
        curve,
        jnp.zeros((12, CELLS), F32),
    ]
    mine = jnp.concatenate(rows, axis=0)
    n = MEMBER_SCALARS
    part_out[n, member] = mine
    part_in[n, member] = mine
    start_parts(n, True)
    parts_like(n).wait_recv()
    total = jnp.sum(part_in[n], axis=0)
    total = jnp.sum(total, axis=1, keepdims=True)
    lane = lax.broadcasted_iota(jnp.int32, (2, CELLS), 1)
    message = jnp.zeros((2, CELLS), F32)
    for i in range(4):
        message = jnp.where(lane == i, total[i : i + 1, :], message)
    for i in range(REGIONS):
        cols_out[SCALARS, i] = message
    cols_in[SCALARS, region] = message
    start_columns(SCALARS)
    columns_like(SCALARS).wait_recv()
    sums = jnp.sum(cols_in[SCALARS], axis=0)[0:1]
    lane = lane[0:1]
    norm, cross, square, bent = (
        jnp.sum(jnp.where(lane == i, sums, 0.0), axis=1, keepdims=True) for i in range(4)
    )
    step = norm / cross
    norm_next = norm - 2.0 * step * cross + step * step * square
    ratio = norm_next / norm
    along = 1.0 + ratio
    image = along * along * cross - 2.0 * along * step * square + step * step * (square + bent)
    step_next = norm_next / image
    out_ref[...] = control_ref[...] + (step + step_next * along) * first - (step_next * step) * second

    for n in range(7):
        columns_like(n).wait_send()
    for n in range(6):
        parts_like(n).wait_send()
    for n in range(5):
        for side in range(2):
            halo(n, side).wait_send()


def local(
    perturbations, control, vertical_loc, block_kernels, loc_pattern, obs_region, obs_slot, obs_cell, innovations,
    obs_weight,
):
    codes = (obs_slot * CELLS + obs_cell + 1).reshape(TILES, CELLS)
    vmem, smem, anywhere = (pl.BlockSpec(memory_space=s) for s in (pltpu.VMEM, pltpu.SMEM, pl.ANY))
    dma = pltpu.SemaphoreType.DMA
    out = pl.pallas_call(
        kernel,
        out_shape=jax.ShapeDtypeStruct((ROWS, CELLS), F32),
        in_specs=[anywhere, vmem, vmem, vmem, smem, vmem, vmem, anywhere, anywhere],
        out_specs=vmem,
        scratch_shapes=[
            pltpu.VMEM((OWN, 2, LEV, CELLS), BF16),
            pltpu.VMEM((TILES, CELLS, CELLS), F32),
            pltpu.VMEM((LPM, TILES * CELLS), F32),
            pltpu.VMEM((ROWS, CELLS), F32),
            pltpu.VMEM((ROWS, CELLS), F32),
            pltpu.VMEM((5, ROWS, CELLS), BF16),
            pltpu.VMEM((5, 2, ROWS, CELLS), BF16),
            pltpu.VMEM((8, CELLS), F32),
            pltpu.VMEM((7, REGIONS, 2, CELLS), F32),
            pltpu.VMEM((7, REGIONS, 2, CELLS), F32),
            pltpu.VMEM((6, MEMBERS, 2 * LPM, CELLS), F32),
            pltpu.VMEM((6, MEMBERS, 2 * LPM, CELLS), F32),
            pltpu.VMEM((2 * CELLS, 16 * CELLS), BF16),
            pltpu.VMEM((2, TILES, 2 * CELLS, 2 * CELLS), BF16),
            pltpu.VMEM((TILES, LPM, 2 * CELLS), F32),
            pltpu.VMEM((2, 3, CELLS, CELLS), BF16),
            pltpu.VMEM((2, 2 * LEV, 2 * LEV), BF16),
            dma((3,)),
            pltpu.SemaphoreType.REGULAR,
            dma((7,)), dma((7,)),
            dma((6,)), dma((6,)),
            dma((5, 2)), dma((5, 2)),
        ],
        compiler_params=pltpu.CompilerParams(collective_id=0, has_side_effects=True, vmem_limit_bytes=40 << 20),
    )(
        perturbations, control.reshape(ROWS, CELLS), vertical_loc, block_kernels, loc_pattern,
        obs_region.reshape(TILES, CELLS), codes, innovations, obs_weight,
    )
    return out.reshape(OWN, LEV, CELLS)


def solution(mesh):
    placed = (
        P("member", None, None, "region"),
        P("member", None, "region"),
        P(),
        P(),
        P(),
        P("region", None),
        P("region"),
        P("region"),
        P(None, "region"),
        P("region", None, None),
    )
    return jax.shard_map(
        local, mesh=mesh, in_specs=placed, out_specs=P("member", None, "region"), check_vma=False
    )
```

time: 707 us -> 149 us (0.21)
  blocking collectives: 551 us -> 0 us
  Pallas kernels: 0 us -> 141 us
  starting transfers between devices: 59.2 us -> 0 us
  waiting for transfers between devices: 48.5 us -> 0 us
  local copies, waits for them, and re-layouts: 19.2 us -> 6.28 us
  matrix products: 11.3 us -> 0 us
  other arithmetic: 10.9 us -> 0.72 us
    psum x9 -> x0, blocking collectives: 462 us -> none  [the longest x2 205 us: squared_norm(): return lax.psum(jnp.sum(vector * vector), ('region', 'member'))]
    pallas_call x0 -> x1, Pallas kernels: none -> 141 us  [local(): pl.pallas_call(kernel, out_shape=jax.ShapeDtypeStruct((ROWS, CELLS), F32)...]
    all_to_all x4 -> x0, blocking collectives: 88.8 us -> none  [the longest x2 54.1 us: apply_operator(): lax.all_to_all(sampled.astype(jnp.bfloat16), 'region', split_axis=1, conc...]
    all_to_all x3 -> x0, starting transfers between devices: 32.5 us -> none  [the longest x1 20.4 us: local(): lax.all_to_all(padded_codes[slot_row], 'region', split_axis=0, concat_axi...]
    all_to_all x3 -> x0, waiting for transfers between devices: 31.4 us -> none  [the longest x1 13.5 us: apply_operator(): lax.all_to_all(returned.astype(jnp.bfloat16), 'region', split_axis=1, con...]
    ppermute x12 -> x0, starting transfers between devices: 26.8 us -> none  [the longest x6 19 us: padded_2(): lax.ppermute(lax.slice_in_dim(block, block.shape[dim] - width, None, axis...]
    ppermute x12 -> x0, waiting for transfers between devices: 17.1 us -> none  [the longest x6 13 us: padded_2(): lax.ppermute(lax.slice_in_dim(block, 0, width, axis=dim), axis, backward)]
    dot_general x29 -> x0, matrix products: 11.3 us -> none  [the longest x5 4.17 us: pick_kernels(): jnp.einsum('bk,kij->bij', onehot, block_kernels, preferred_element_type=j...]
  transfers between devices with their start and end apart: 15 -> 0, of which waited for: 13 -> 0; matrix products, arithmetic and copies ran while one was open for 2% -> 0% of each run, Pallas kernels for 0% -> 0%
where the time goes in v1:
time: 149 us; the launch traced here: 148 us
  Pallas kernels  141 us (95%)
  local copies, waits for them, and re-layouts  6.28 us (4%)
    pallas_call x1, Pallas kernels, local(): pl.pallas_call(kernel, out_shape=jax.ShapeDtypeStruct((ROWS, CELLS), F32)...  141 us
    unnamed x18, local copies, waits for them, and re-layouts  6.28 us

profile of v1, /device:TPU:1, one launch (start us, length us, event | category | flops | bytes accessed | tf_op | source)
XLA Modules:
  0.0 148.3 jit_solution(16499464194837720835)
XLA Ops:
  0.0 0.0 copy-start.7
  0.0 0.7 add_bitcast_fusion.code_ref
  0.7 0.0 copy-done.7
  0.7 0.0 copy-start.5
  0.7 0.0 copy-start.6
  0.7 0.1 copy.11.pattern_ref
  0.8 0.6 copy-done.5
  1.4 0.0 copy-done.6
  1.4 0.0 copy-start
  1.4 1.0 copy-done
  2.5 0.0 copy-start.1
  2.5 1.0 copy-done.1
  3.5 0.0 copy-start.2
  3.5 1.0 copy-done.2
  4.4 0.0 copy-start.3
  4.4 0.9 copy-done.3
  5.4 0.0 copy-start.4
  5.4 0.9 copy-done.4
  6.3 141.3 %shard_map.100 = f32[640,128]{1,0:T(8,128)S(1)} custom-call(bf16[10,2,64,128]{3,2,1,0:T(8,128)(2,1)S(1)} %copy-done.1, f32[640,128]{1,0:T(8,128)S(1)} %bitcast.6, bf16[64,64]{1,0:T(8,128)(2,1)S(1)} %copy-done.5, bf16[4,128,128]{2,1,0:T(8,128)(2,1)S(1)} %copy-done.4, s32[64,3]{1,0:T(8,128)S(1)} %copy.11.pattern_ref, s32[8,128]{1,0:T(8,128)S(1)} %bitcast.7, ...), custom_call_target="tpu_custom_call" | custom-call | tf_op jit(solution)/shard_map/pallas_call | solution.py:383
  147.6 0.7 copy.13
Async XLA Ops:
  0.0 0.7 copy-start.7
  0.7 0.7 copy-start.5
  0.7 0.7 copy-start.6
  1.4 1.0 copy-start
  2.5 1.0 copy-start.1
  3.5 1.0 copy-start.2
  4.4 0.9 copy-start.3
  5.4 0.9 copy-start.4

commit v2 on v1

v2 whole, which is shorter than its diff:
```python
import jax
import jax.numpy as jnp
from jax import lax
from jax.experimental import pallas as pl
from jax.experimental.pallas import tpu as pltpu
from jax.sharding import PartitionSpec as P

REGIONS, MEMBERS = 64, 8
OWN = 10
LEV, CELLS = 64, 128
ROWS = OWN * LEV
TILES = 8
LPM = LEV // MEMBERS
KTYPES = 4
CHUNKS = OWN // 2
CHUNK = ROWS // CHUNKS
EARLY = 2
F32, BF16 = jnp.float32, jnp.bfloat16
MESH = pl.DeviceIdType.MESH
CODES, SAMPLES, RETURNS, SCALARS = 0, (1, 3, 5), (2, 4), 6
SUMS, ADJOINTS, MEMBER_SCALARS = (0, 2, 4), (1, 3), 5
VECTORS, LIFTED = (0, 2, 4), (1, 3)


def dot(a, b):
    return jnp.dot(a, b, preferred_element_type=F32)


def dot_nt(a, b):
    return lax.dot_general(a, b, (((1,), (1,)), ((), ())), preferred_element_type=F32)


def bit_of(shape, axis, stride):
    return (lax.broadcasted_iota(jnp.int32, shape, axis) & stride) != 0


def swap_bits(x, row_stride, lane_stride):
    n = x.shape[0]
    row, lane = bit_of(x.shape, 0, row_stride), bit_of(x.shape, 1, lane_stride)
    up = pltpu.roll(pltpu.roll(x, n - row_stride, 0), lane_stride, 1)
    down = pltpu.roll(pltpu.roll(x, row_stride, 0), CELLS - lane_stride, 1)
    return jnp.where(row == lane, x, jnp.where(row, down, up))


def region_major(x):
    return swap_bits(swap_bits(x, 2, 32), 4, 64)


def tile_major(x):
    return swap_bits(swap_bits(swap_bits(x, 8, 4), 16, 8), 32, 16)


def split(x):
    high = x.astype(BF16)
    return high, (x - high.astype(F32)).astype(BF16)


def kernel(
    pert_hbm, control_hbm, vloc_hbm, table_hbm, pattern_hbm, region_hbm, slot_hbm, cell_hbm, innov_hbm, weight_hbm,
    out_ref,
    pert, control, vloc_ref, table, pattern, obs, weight, innov, r0, q, halo_out, halo_in,
    cols_out, cols_in, sums_out, sums_in, part_out, part_in,
    placing, onehot, coupling, innov_slots, blocks, vert,
    load_sem, col_send, col_recv, part_send, part_recv, halo_send, halo_recv,
):
    region, member = lax.axis_index("region"), lax.axis_index("member")
    left, right = lax.rem(region + (REGIONS - 1), REGIONS), lax.rem(region + 1, REGIONS)

    here = pl.multiple_of(member * LPM, LPM)
    pairs = [
        (region_hbm, obs.at[0]),
        (slot_hbm, obs.at[1]),
        (cell_hbm, obs.at[2]),
        (control_hbm, control),
        (table_hbm, table),
        (vloc_hbm, vloc_ref),
        (weight_hbm, weight),
        (innov_hbm.at[pl.ds(here, LPM)], innov),
        (pert_hbm, pert),
        (pattern_hbm, pattern),
    ]
    loads = [pltpu.make_async_copy(a, b, load_sem.at[i]) for i, (a, b) in enumerate(pairs)]
    barrier = pltpu.get_barrier_semaphore()

    def greet(i):
        pl.semaphore_signal(
            barrier, inc=1, device_id={"region": lax.rem(region + i, REGIONS)}, device_id_type=MESH
        )

    def greet_pair(i, _):
        greet(32 - i)
        greet(32 + i)
        return 0

    greet(32)
    lax.fori_loop(1, 32, greet_pair, 0)

    def greet_member(i, _):
        pl.semaphore_signal(
            barrier, inc=1, device_id={"member": lax.rem(member + i, MEMBERS)}, device_id_type=MESH
        )
        return 0

    lax.fori_loop(1, MEMBERS, greet_member, 0)
    for load in loads:
        load.start()

    def buffers(n):
        return (sums_out, sums_in) if n == SCALARS else (cols_out.at[n], cols_in.at[n])

    def start_columns(n):
        source, target = buffers(n)

        def one(i):
            to = lax.rem(region + i, REGIONS)
            pltpu.make_async_remote_copy(
                src_ref=source.at[to], dst_ref=target.at[region],
                send_sem=col_send.at[n], recv_sem=col_recv.at[n],
                device_id={"region": to}, device_id_type=MESH,
            ).start()

        def pair(j, _):
            one(32 - j)
            one(32 + j)
            return 0

        one(32)
        lax.fori_loop(1, 32, pair, 0)

    def columns_like(n):
        source, target = buffers(n)
        return pltpu.make_async_remote_copy(
            src_ref=source.at[pl.ds(0, REGIONS - 1)], dst_ref=target.at[pl.ds(0, REGIONS - 1)],
            send_sem=col_send.at[n], recv_sem=col_recv.at[n],
            device_id={"region": right}, device_id_type=MESH,
        )

    def start_parts(n, same):
        def one(i, _):
            to = lax.rem(member + i, MEMBERS)
            pltpu.make_async_remote_copy(
                src_ref=part_out.at[n, member if same else to], dst_ref=part_in.at[n, member],
                send_sem=part_send.at[n], recv_sem=part_recv.at[n],
                device_id={"member": to}, device_id_type=MESH,
            ).start()
            return 0

        lax.fori_loop(1, MEMBERS, one, 0)

    def parts_like(n):
        return pltpu.make_async_remote_copy(
            src_ref=part_out.at[n, pl.ds(0, MEMBERS - 1)], dst_ref=part_in.at[n, pl.ds(0, MEMBERS - 1)],
            send_sem=part_send.at[n], recv_sem=part_recv.at[n],
            device_id={"member": lax.rem(member + 1, MEMBERS)}, device_id_type=MESH,
        )

    def halo(n, side, chunk):
        rows = pl.ds(CHUNK * chunk, CHUNK)
        return pltpu.make_async_remote_copy(
            src_ref=halo_out.at[n, rows], dst_ref=halo_in.at[n, 1 - side, rows],
            send_sem=halo_send.at[n, side, chunk], recv_sem=halo_recv.at[n, 1 - side, chunk],
            device_id={"region": left if side == 0 else right}, device_id_type=MESH,
        )

    def send_halo(n, chunk, x):
        halo_out[n, CHUNK * chunk : CHUNK * (chunk + 1)] = x
        for side in range(2):
            halo(n, side, chunk).start()

    def wait_halo(n, chunk):
        rows = pl.ds(CHUNK * chunk, CHUNK)
        for side in range(2):
            pltpu.make_async_remote_copy(
                src_ref=halo_out.at[n, rows], dst_ref=halo_in.at[n, side, rows],
                send_sem=halo_send.at[n, 1 - side, chunk], recv_sem=halo_recv.at[n, side, chunk],
                device_id={"region": left if side == 0 else right}, device_id_type=MESH,
            ).wait_recv()

    def send_columns(n, x):
        cols_out[n] = region_major(x).astype(BF16).reshape(REGIONS, 2, CELLS)
        cols_in[n, region] = cols_out[n, region]
        start_columns(n)

    def get_columns(n):
        columns_like(n).wait_recv()
        return region_major(cols_in[n].reshape(2 * REGIONS, CELLS).astype(F32))

    for load in loads[:3]:
        load.wait()
    regions8 = obs[0]
    codes8 = (obs[1] * CELLS + obs[2] + 1).astype(F32).astype(BF16)
    iota_row = lax.broadcasted_iota(jnp.int32, (CELLS, CELLS), 0)
    iota_lane = lax.broadcasted_iota(jnp.int32, (CELLS, CELLS), 1)
    identity = (iota_row == iota_lane).astype(F32).astype(BF16)
    zz, xx = regions8 >> 2, regions8 & 3
    base8 = 128 * (zz >> 3) + 32 * xx + 4 * (zz & 7)
    base_cols = dot_nt(identity, base8.astype(F32).astype(BF16)).astype(jnp.int32)
    slot_lane = lax.broadcasted_iota(jnp.int32, (CELLS, 2 * CELLS), 1)
    slot_row = lax.broadcasted_iota(jnp.int32, (2 * CELLS, CELLS), 0)
    tile_rows = lax.broadcasted_iota(jnp.int32, (8, 2 * CELLS), 0)
    code_halves = [[], []]
    for t in range(TILES):
        col, row = base_cols[:, t : t + 1], base8[t : t + 1, :]
        same = col == row
        rank = jnp.sum((same & (iota_lane < iota_row)).astype(F32), axis=1, keepdims=True)
        place = (slot_lane == col + rank.astype(jnp.int32)).astype(F32).astype(BF16)
        placing[t] = place
        codes = dot(codes8, place)
        codes = jnp.sum(jnp.where(tile_rows == t, codes, 0.0), axis=0, keepdims=True)
        codes = jnp.broadcast_to(codes, (8, 2 * CELLS))
        code_halves[0].append(codes[:, :CELLS])
        code_halves[1].append(codes[:, CELLS:])
    code_rows = tile_major(jnp.concatenate(code_halves[0] + code_halves[1], axis=0))
    loads[3].wait()

    pl.semaphore_wait(barrier, REGIONS - 1 + MEMBERS - 1)
    for chunk in range(CHUNKS):
        send_halo(VECTORS[0], chunk, control[CHUNK * chunk : CHUNK * (chunk + 1)].astype(BF16))
    send_columns(CODES, code_rows)

    loads[4].wait()
    loads[5].wait()
    loads[9].wait()

    block_lane = lax.broadcasted_iota(jnp.int32, (1, REGIONS), 1)

    def block_of(at, offset):
        found = jnp.where(block_lane == at, pattern[offset : offset + 1, :].astype(F32), 0.0)
        entry = jnp.sum(found, axis=1, keepdims=True)
        total = jnp.zeros((CELLS, CELLS), F32)
        for k in range(KTYPES):
            total = total + table[k].astype(F32) * (entry == k).astype(F32)
        return total * ((at >= 0) & (at < REGIONS)).astype(F32)

    for side in range(3):
        present = (region + side - 1 >= 0) & (region + side - 1 < REGIONS)
        blocks[0, side] = (block_of(region, side) * present.astype(F32)).astype(BF16)
        blocks[1, side] = dot_nt(identity, block_of(region + side - 1, 2 - side).astype(BF16)).astype(BF16)
    zeros = jnp.zeros((LEV, LEV), BF16)
    vloc = vloc_ref[...]
    vloc_t = dot_nt(identity[:LEV, :LEV], vloc).astype(BF16)
    for i, v in enumerate((vloc, vloc_t)):
        vert[i] = jnp.concatenate(
            [jnp.concatenate([v, zeros], axis=1), jnp.concatenate([zeros, v], axis=1)], axis=0
        )
    loads[8].wait()
    loads[6].wait()
    loads[7].wait()

    def couple(t):
        row = base8[t : t + 1, :]
        same = base_cols[:, t : t + 1] == row
        rank = jnp.sum((same & (iota_row < iota_lane)).astype(F32), axis=0, keepdims=True)
        place_t = (slot_row == row + rank.astype(jnp.int32)).astype(F32).astype(BF16)
        place = placing[t]
        for i, part in enumerate(split(weight[t])):
            coupling[i, t] = dot(place_t, dot(part, place).astype(BF16)).astype(BF16)
        high, low = split(innov[:, CELLS * t : CELLS * (t + 1)])
        innov_slots[t] = dot(high, place) + dot(low, place)

    def make_onehot():
        codes = get_columns(CODES)
        code_row = lax.broadcasted_iota(jnp.int32, (2 * CELLS, CELLS), 0)
        for z in range(16):
            want = codes[8 * z : 8 * z + 1, :].astype(jnp.int32) - 1
            onehot[:, CELLS * z : CELLS * (z + 1)] = (code_row == want).astype(F32).astype(BF16)

    def conv(which, n, chunk):
        rows = slice(CHUNK * chunk, CHUNK * (chunk + 1))
        return (
            dot(halo_in[n, 0, rows], blocks[which, 0])
            + dot(halo_out[n, rows], blocks[which, 1])
            + dot(halo_in[n, 1, rows], blocks[which, 2])
        )

    def forward(it):
        sums = [jnp.zeros((LEV, CELLS), F32) for _ in range(2)]
        for chunk in range(CHUNKS):
            wait_halo(VECTORS[it], chunk)
            local = dot(vert[0], conv(0, VECTORS[it], chunk).astype(BF16))
            for i in range(2):
                for s in range(2):
                    sums[s] = sums[s] + pert[2 * chunk + i, s].astype(F32) * local[LEV * i : LEV * (i + 1)]
        n = SUMS[it]
        for to in range(MEMBERS):
            for s in range(2):
                part_out[n, to, LPM * s : LPM * (s + 1)] = sums[s][LPM * to : LPM * (to + 1)]
        part_in[n, member] = part_out[n, member]
        start_parts(n, False)
        if it == 0:
            for t in range(EARLY):
                couple(t)
            make_onehot()
        parts_like(n).wait_recv()
        total = jnp.sum(part_in[n], axis=0)
        increment = jnp.concatenate([total[:LPM], total[LPM:]], axis=1).astype(BF16)
        sampled = dot(increment, onehot[...])
        send_columns(
            SAMPLES[it], jnp.concatenate([sampled[:, CELLS * z : CELLS * (z + 1)] for z in range(16)], axis=0)
        )
        if it == 0:
            for t in range(EARLY, TILES):
                couple(t)

    def weighted(it):
        slots = tile_major(get_columns(SAMPLES[it]))
        departures, results = [], []
        for t in range(TILES):
            here = jnp.concatenate([slots[8 * t : 8 * t + 8], slots[64 + 8 * t : 72 + 8 * t]], axis=1)
            if it == 0:
                here = here - innov_slots[t]
                high, low = split(here)
                result = dot(high, coupling[0, t]) + dot(low, coupling[0, t]) + dot(high, coupling[1, t])
            else:
                high = here.astype(BF16)
                result = dot(high, coupling[0, t]) + dot(high, coupling[1, t])
            departures.append(here)
            results.append(result)
        return departures, results

    def backward(it, results, update):
        back = jnp.concatenate([x[:, :CELLS] for x in results] + [x[:, CELLS:] for x in results], axis=0)
        send_columns(RETURNS[it], tile_major(back))
        here = get_columns(RETURNS[it]).astype(BF16)
        here = jnp.concatenate([here[8 * z : 8 * z + 8] for z in range(16)], axis=1)
        adjoint = dot_nt(here, onehot[...])
        n = ADJOINTS[it]
        mine = jnp.concatenate([adjoint[:, :CELLS], adjoint[:, CELLS:]], axis=0)
        part_out[n, member] = mine
        part_in[n, member] = mine
        start_parts(n, True)
        parts_like(n).wait_recv()
        fields = part_in[n]
        fields = [fields[:, LPM * s : LPM * (s + 1)].reshape(LEV, CELLS) for s in range(2)]
        for chunk in range(CHUNKS):
            projected = jnp.concatenate(
                [
                    pert[k, 0].astype(F32) * fields[0] + pert[k, 1].astype(F32) * fields[1]
                    for k in (2 * chunk, 2 * chunk + 1)
                ],
                axis=0,
            ).astype(BF16)
            send_halo(LIFTED[it], chunk, dot(vert[1], projected).astype(BF16))
        for chunk in range(CHUNKS):
            wait_halo(LIFTED[it], chunk)
            update(chunk, slice(CHUNK * chunk, CHUNK * (chunk + 1)), conv(1, LIFTED[it], chunk))

    def residual(chunk, rows, back):
        value = -(control[rows] + back)
        r0[rows] = value
        send_halo(VECTORS[1], chunk, value.astype(BF16))

    forward(0)
    _, results = weighted(0)
    backward(0, results, residual)

    def image_of(chunk, rows, back):
        value = r0[rows] + back
        q[rows] = value
        send_halo(VECTORS[2], chunk, value.astype(BF16))

    forward(1)
    _, results = weighted(1)
    backward(1, results, image_of)

    forward(2)
    departures, results = weighted(2)
    curve = sum(jnp.sum(d * w, axis=0, keepdims=True) for d, w in zip(departures, results, strict=True))
    curve = curve[:, :CELLS] + curve[:, CELLS:]
    first, second = r0[...], q[...]
    rows = [
        jnp.sum(first * first, axis=0, keepdims=True),
        jnp.sum(first * second, axis=0, keepdims=True),
        jnp.sum(second * second, axis=0, keepdims=True),
        curve,
        jnp.zeros((12, CELLS), F32),
    ]
    mine = jnp.concatenate(rows, axis=0)
    n = MEMBER_SCALARS
    part_out[n, member] = mine
    part_in[n, member] = mine
    start_parts(n, True)
    parts_like(n).wait_recv()
    total = jnp.sum(part_in[n], axis=0)
    total = jnp.sum(total, axis=1, keepdims=True)
    lane = lax.broadcasted_iota(jnp.int32, (1, CELLS), 1)
    message = jnp.zeros((1, CELLS), F32)
    for i in range(4):
        message = jnp.where(lane == i, total[i : i + 1, :], message)
    sums_out[...] = jnp.broadcast_to(message[None], (REGIONS, 1, CELLS))
    sums_in[region] = message
    start_columns(SCALARS)
    columns_like(SCALARS).wait_recv()
    sums = jnp.sum(sums_in[...], axis=0)
    norm, cross, square, bent = (
        jnp.sum(jnp.where(lane == i, sums, 0.0), axis=1, keepdims=True) for i in range(4)
    )
    step = norm / cross
    norm_next = norm - 2.0 * step * cross + step * step * square
    ratio = norm_next / norm
    along = 1.0 + ratio
    image = along * along * cross - 2.0 * along * step * square + step * step * (square + bent)
    step_next = norm_next / image
    out_ref[...] = control[...] + (step + step_next * along) * first - (step_next * step) * second

    for n in range(7):
        columns_like(n).wait_send()
    for n in range(6):
        parts_like(n).wait_send()
    for n in range(5):
        for side in range(2):
            for chunk in range(CHUNKS):
                halo(n, side, chunk).wait_send()


def local(
    perturbations, control, vertical_loc, block_kernels, loc_pattern, obs_region, obs_slot, obs_cell, innovations,
    obs_weight,
):
    vmem, hbm = (pl.BlockSpec(memory_space=s) for s in (pltpu.VMEM, pltpu.HBM))
    dma = pltpu.SemaphoreType.DMA
    out = pl.pallas_call(
        kernel,
        out_shape=jax.ShapeDtypeStruct((ROWS, CELLS), F32),
        in_specs=[hbm] * 10,
        out_specs=vmem,
        scratch_shapes=[
            pltpu.VMEM((OWN, 2, LEV, CELLS), BF16),
            pltpu.VMEM((ROWS, CELLS), F32),
            pltpu.VMEM((LEV, LEV), BF16),
            pltpu.VMEM((KTYPES, CELLS, CELLS), BF16),
            pltpu.VMEM((3, REGIONS), jnp.int32),
            pltpu.VMEM((3, TILES, CELLS), jnp.int32),
            pltpu.VMEM((TILES, CELLS, CELLS), F32),
            pltpu.VMEM((LPM, TILES * CELLS), F32),
            pltpu.VMEM((ROWS, CELLS), F32),
            pltpu.VMEM((ROWS, CELLS), F32),
            pltpu.VMEM((5, ROWS, CELLS), BF16),
            pltpu.VMEM((5, 2, ROWS, CELLS), BF16),
            pltpu.VMEM((6, REGIONS, 2, CELLS), BF16),
            pltpu.VMEM((6, REGIONS, 2, CELLS), BF16),
            pltpu.VMEM((REGIONS, 1, CELLS), F32),
            pltpu.VMEM((REGIONS, 1, CELLS), F32),
            pltpu.VMEM((6, MEMBERS, 2 * LPM, CELLS), F32),
            pltpu.VMEM((6, MEMBERS, 2 * LPM, CELLS), F32),
            pltpu.VMEM((TILES, CELLS, 2 * CELLS), BF16),
            pltpu.VMEM((2 * CELLS, 16 * CELLS), BF16),
            pltpu.VMEM((2, TILES, 2 * CELLS, 2 * CELLS), BF16),
            pltpu.VMEM((TILES, LPM, 2 * CELLS), F32),
            pltpu.VMEM((2, 3, CELLS, CELLS), BF16),
            pltpu.VMEM((2, 2 * LEV, 2 * LEV), BF16),
            dma((10,)),
            dma((7,)), dma((7,)),
            dma((6,)), dma((6,)),
            dma((5, 2, CHUNKS)), dma((5, 2, CHUNKS)),
        ],
        compiler_params=pltpu.CompilerParams(collective_id=0, has_side_effects=True, vmem_limit_bytes=60 << 20),
    )(
        perturbations, control.reshape(ROWS, CELLS), vertical_loc, block_kernels, loc_pattern.T,
        obs_region.reshape(TILES, CELLS), obs_slot.reshape(TILES, CELLS), obs_cell.reshape(TILES, CELLS),
        innovations, obs_weight,
    )
    return out.reshape(OWN, LEV, CELLS)


def solution(mesh):
    placed = (
        P("member", None, None, "region"),
        P("member", None, "region"),
        P(),
        P(),
        P(),
        P("region", None),
        P("region"),
        P("region"),
        P(None, "region"),
        P("region", None, None),
    )
    return jax.shard_map(
        local, mesh=mesh, in_specs=placed, out_specs=P("member", None, "region"), check_vma=False
    )
```

time: 149 us -> 131 us (0.88)
  Pallas kernels: 141 us -> 130 us
  local copies, waits for them, and re-layouts: 6.28 us -> 1.72 us
    pallas_call x1, Pallas kernels: 141 us -> 130 us  [local(): pl.pallas_call(kernel, out_shape=jax.ShapeDtypeStruct((ROWS, CELLS), F32)...]
    unnamed x18 -> x1, local copies, waits for them, and re-layouts: 6.28 us -> 1.72 us
where the time goes in v2:
time: 131 us
  Pallas kernels  130 us (99%)
  local copies, waits for them, and re-layouts  1.72 us (1%)
    pallas_call x1, Pallas kernels, local(): pl.pallas_call(kernel, out_shape=jax.ShapeDtypeStruct((ROWS, CELLS), F32)...  130 us

profile of v2, /device:TPU:1, one launch (start us, length us, event | category | flops | bytes accessed | tf_op | source)
XLA Modules:
  0.0 131.3 jit_solution(6507298159734005940)
XLA Ops:
  0.0 129.5 %shard_map.100 = f32[640,128]{1,0:T(8,128)} custom-call(bf16[10,2,64,128]{3,2,1,0:T(8,128)(2,1)} %pert_hbm.1, f32[640,128]{1,0:T(8,128)} %bitcast.7, bf16[64,64]{1,0:T(8,128)(2,1)} %vloc_hbm.1, bf16[4,128,128]{2,1,0:T(8,128)(2,1)} %table_hbm.1, s32[3,64]{1,0:T(4,128)} %bitcast.11, s32[8,128]{1,0:T(8,128)} %bitcast.8, s32[8,128]{1,0:T(8,128)} %bitcast.9, ...), custom_call_target="tpu_custom_call" | custom-call | tf_op jit(solution)/shard_map/pallas_call | solution.py:422
  129.5 1.7 %copy.12 = f32[10,64,128]{2,1,0:T(8,128)} copy(f32[10,64,128]{2,1,0:T(8,128)} %bitcast.6) | data formatting | bytes 655360

commit v3 on v2

--- a/solution.py
+++ b/solution.py
@@ -60,7 +60,7 @@
     out_ref,
     pert, control, vloc_ref, table, pattern, obs, weight, innov, r0, q, halo_out, halo_in,
     cols_out, cols_in, sums_out, sums_in, part_out, part_in,
-    placing, onehot, coupling, innov_slots, blocks, vert,
+    placing, onehot, onehot_t, coupling, innov_slots, blocks, vert,
     load_sem, col_send, col_recv, part_send, part_recv, halo_send, halo_recv,
 ):
     region, member = lax.axis_index("region"), lax.axis_index("member")
@@ -176,9 +176,12 @@
                 device_id={"region": left if side == 0 else right}, device_id_type=MESH,
             ).wait_recv()
 
-    def send_columns(n, x):
+    def stage_columns(n, x):
         cols_out[n] = region_major(x).astype(BF16).reshape(REGIONS, 2, CELLS)
         cols_in[n, region] = cols_out[n, region]
+
+    def send_columns(n, x):
+        stage_columns(n, x)
         start_columns(n)
 
     def get_columns(n):
@@ -211,12 +214,15 @@
         code_halves[0].append(codes[:, :CELLS])
         code_halves[1].append(codes[:, CELLS:])
     code_rows = tile_major(jnp.concatenate(code_halves[0] + code_halves[1], axis=0))
+    stage_columns(CODES, code_rows)
     loads[3].wait()
+    halo_out[VECTORS[0]] = control[...].astype(BF16)
 
     pl.semaphore_wait(barrier, REGIONS - 1 + MEMBERS - 1)
     for chunk in range(CHUNKS):
-        send_halo(VECTORS[0], chunk, control[CHUNK * chunk : CHUNK * (chunk + 1)].astype(BF16))
-    send_columns(CODES, code_rows)
+        for side in range(2):
+            halo(VECTORS[0], side, chunk).start()
+    start_columns(CODES)
 
     loads[4].wait()
     loads[5].wait()
@@ -258,8 +264,14 @@
         high, low = split(innov[:, CELLS * t : CELLS * (t + 1)])
         innov_slots[t] = dot(high, place) + dot(low, place)
 
-    def make_onehot():
-        codes = get_columns(CODES)
+    def make_onehot_t(codes):
+        cols = dot_nt(identity, codes.reshape(16, 8, CELLS)[:, 0].astype(BF16)).astype(jnp.int32) - 1
+        code_lane = lax.broadcasted_iota(jnp.int32, (CELLS, 2 * CELLS), 1)
+        for z in range(16):
+            hit = (code_lane == cols[:, z : z + 1]).astype(F32).astype(BF16)
+            onehot_t[CELLS * z : CELLS * (z + 1)] = hit
+
+    def make_onehot(codes):
         code_row = lax.broadcasted_iota(jnp.int32, (2 * CELLS, CELLS), 0)
         for z in range(16):
             want = codes[8 * z : 8 * z + 1, :].astype(jnp.int32) - 1
@@ -290,7 +302,8 @@
         if it == 0:
             for t in range(EARLY):
                 couple(t)
-            make_onehot()
+            codes = get_columns(CODES)
+            make_onehot(codes)
         parts_like(n).wait_recv()
         total = jnp.sum(part_in[n], axis=0)
         increment = jnp.concatenate([total[:LPM], total[LPM:]], axis=1).astype(BF16)
@@ -301,6 +314,7 @@
         if it == 0:
             for t in range(EARLY, TILES):
                 couple(t)
+            make_onehot_t(codes)
 
     def weighted(it):
         slots = tile_major(get_columns(SAMPLES[it]))
@@ -310,10 +324,13 @@
             if it == 0:
                 here = here - innov_slots[t]
                 high, low = split(here)
-                result = dot(high, coupling[0, t]) + dot(low, coupling[0, t]) + dot(high, coupling[1, t])
-            else:
+                both = dot(jnp.concatenate([high, low], axis=0), coupling[0, t])
+                result = both[:LPM] + both[LPM:] + dot(high, coupling[1, t])
+            elif it == 1:
                 high = here.astype(BF16)
                 result = dot(high, coupling[0, t]) + dot(high, coupling[1, t])
+            else:
+                result = dot(here.astype(BF16), coupling[0, t])
             departures.append(here)
             results.append(result)
         return departures, results
@@ -323,7 +340,7 @@
         send_columns(RETURNS[it], tile_major(back))
         here = get_columns(RETURNS[it]).astype(BF16)
         here = jnp.concatenate([here[8 * z : 8 * z + 8] for z in range(16)], axis=1)
-        adjoint = dot_nt(here, onehot[...])
+        adjoint = dot(here, onehot_t[...])
         n = ADJOINTS[it]
         mine = jnp.concatenate([adjoint[:, :CELLS], adjoint[:, CELLS:]], axis=0)
         part_out[n, member] = mine
@@ -445,6 +462,7 @@
             pltpu.VMEM((6, MEMBERS, 2 * LPM, CELLS), F32),
             pltpu.VMEM((TILES, CELLS, 2 * CELLS), BF16),
             pltpu.VMEM((2 * CELLS, 16 * CELLS), BF16),
+            pltpu.VMEM((16 * CELLS, 2 * CELLS), BF16),
             pltpu.VMEM((2, TILES, 2 * CELLS, 2 * CELLS), BF16),
             pltpu.VMEM((TILES, LPM, 2 * CELLS), F32),
             pltpu.VMEM((2, 3, CELLS, CELLS), BF16),

time: 131 us -> 131 us (level)
  no operation moved by 1% of the time
where the time goes in v3:
time: 131 us
  Pallas kernels  129 us (98%)
  local copies, waits for them, and re-layouts  1.72 us (1%)
    pallas_call x1, Pallas kernels, local(): pl.pallas_call(kernel, out_shape=jax.ShapeDtypeStruct((ROWS, CELLS), F32)...  129 us

profile of v3, /device:TPU:1, one launch (start us, length us, event | category | flops | bytes accessed | tf_op | source)
XLA Modules:
  0.0 130.5 jit_solution(17977755394599543797)
XLA Ops:
  0.0 128.8 %shard_map.100 = f32[640,128]{1,0:T(8,128)} custom-call(bf16[10,2,64,128]{3,2,1,0:T(8,128)(2,1)} %pert_hbm.1, f32[640,128]{1,0:T(8,128)} %bitcast.7, bf16[64,64]{1,0:T(8,128)(2,1)} %vloc_hbm.1, bf16[4,128,128]{2,1,0:T(8,128)(2,1)} %table_hbm.1, s32[3,64]{1,0:T(4,128)} %bitcast.11, s32[8,128]{1,0:T(8,128)} %bitcast.8, s32[8,128]{1,0:T(8,128)} %bitcast.9, ...), custom_call_target="tpu_custom_call" | custom-call | tf_op jit(solution)/shard_map/pallas_call | solution.py:439
  128.8 1.7 %copy.12 = f32[10,64,128]{2,1,0:T(8,128)} copy(f32[10,64,128]{2,1,0:T(8,128)} %bitcast.6) | data formatting | bytes 655360

commit v4 on v3

--- a/solution.py
+++ b/solution.py
@@ -58,7 +58,7 @@
 def kernel(
     pert_hbm, control_hbm, vloc_hbm, table_hbm, pattern_hbm, region_hbm, slot_hbm, cell_hbm, innov_hbm, weight_hbm,
     out_ref,
-    pert, control, vloc_ref, table, pattern, obs, weight, innov, r0, q, halo_out, halo_in,
+    pert, control, vloc_ref, table, pattern, obs, weight, innov, r0, q, own, halo_out, halo_in,
     cols_out, cols_in, sums_out, sums_in, part_out, part_in,
     placing, onehot, onehot_t, coupling, innov_slots, blocks, vert,
     load_sem, col_send, col_recv, part_send, part_recv, halo_send, halo_recv,
@@ -277,15 +277,19 @@
             want = codes[8 * z : 8 * z + 1, :].astype(jnp.int32) - 1
             onehot[:, CELLS * z : CELLS * (z + 1)] = (code_row == want).astype(F32).astype(BF16)
 
+    def own_block(which, n):
+        own[...] = dot(halo_out[n], blocks[which, 1])
+
     def conv(which, n, chunk):
         rows = slice(CHUNK * chunk, CHUNK * (chunk + 1))
         return (
             dot(halo_in[n, 0, rows], blocks[which, 0])
-            + dot(halo_out[n, rows], blocks[which, 1])
+            + own[rows]
             + dot(halo_in[n, 1, rows], blocks[which, 2])
         )
 
     def forward(it):
+        own_block(0, VECTORS[it])
         sums = [jnp.zeros((LEV, CELLS), F32) for _ in range(2)]
         for chunk in range(CHUNKS):
             wait_halo(VECTORS[it], chunk)
@@ -358,6 +362,7 @@
                 axis=0,
             ).astype(BF16)
             send_halo(LIFTED[it], chunk, dot(vert[1], projected).astype(BF16))
+        own_block(1, LIFTED[it])
         for chunk in range(CHUNKS):
             wait_halo(LIFTED[it], chunk)
             update(chunk, slice(CHUNK * chunk, CHUNK * (chunk + 1)), conv(1, LIFTED[it], chunk))
@@ -452,6 +457,7 @@
             pltpu.VMEM((LPM, TILES * CELLS), F32),
             pltpu.VMEM((ROWS, CELLS), F32),
             pltpu.VMEM((ROWS, CELLS), F32),
+            pltpu.VMEM((ROWS, CELLS), F32),
             pltpu.VMEM((5, ROWS, CELLS), BF16),
             pltpu.VMEM((5, 2, ROWS, CELLS), BF16),
             pltpu.VMEM((6, REGIONS, 2, CELLS), BF16),

time: 131 us -> 131 us (level)
  no operation moved by 1% of the time
where the time goes in v4:
time: 131 us; the launch traced here: 130 us
  Pallas kernels  129 us (98%)
  local copies, waits for them, and re-layouts  1.72 us (1%)
    pallas_call x1, Pallas kernels, local(): pl.pallas_call(kernel, out_shape=jax.ShapeDtypeStruct((ROWS, CELLS), F32)...  129 us

profile of v4, /device:TPU:1, one launch (start us, length us, event | category | flops | bytes accessed | tf_op | source)
XLA Modules:
  0.0 130.5 jit_solution(12806968813699448097)
XLA Ops:
  0.0 128.8 %shard_map.100 = f32[640,128]{1,0:T(8,128)} custom-call(bf16[10,2,64,128]{3,2,1,0:T(8,128)(2,1)} %pert_hbm.1, f32[640,128]{1,0:T(8,128)} %bitcast.7, bf16[64,64]{1,0:T(8,128)(2,1)} %vloc_hbm.1, bf16[4,128,128]{2,1,0:T(8,128)(2,1)} %table_hbm.1, s32[3,64]{1,0:T(4,128)} %bitcast.11, s32[8,128]{1,0:T(8,128)} %bitcast.8, s32[8,128]{1,0:T(8,128)} %bitcast.9, ...), custom_call_target="tpu_custom_call" | custom-call | tf_op jit(solution)/shard_map/pallas_call | solution.py:444
  128.8 1.7 %copy.12 = f32[10,64,128]{2,1,0:T(8,128)} copy(f32[10,64,128]{2,1,0:T(8,128)} %bitcast.6) | data formatting | bytes 655360
